TPU v7x, 256 devices: a whole 4x4x8 slice. The times are simulated.
256 devices in a mesh: scen: 2 (over core), tx: 8 (over y, x_lo), ty: 16 (over x_hi, z).
Axes of the slice: x: 4 (x_hi: 2, x_lo: 2; x = x_hi * 2 + x_lo), y: 4, z: 8, core: 2. Of those that a mesh axis runs over, the one named last changes fastest.
Arguments:
- conductivity: float32 [512, 512, 128], P('tx', 'ty'), may hold values from 0.1 to 1
- cooling: float32 [2, 512, 512, 128], P('scen', 'tx', 'ty'), may hold values from 0.2 to 1.5
- source: float32 [2, 512, 512, 128], P('scen', 'tx', 'ty'), may hold values from -6 to 6
- adjoint_in: float32 [2, 512, 512, 128], P('scen', 'tx', 'ty'), may hold values from -6 to 6
- store: float32 [2, 6, 128, 128, 2048], P('scen', None, ('tx', 'ty')), may hold values from -6 to 6
- holder: int32 [128, 128], P(('tx', 'ty')), may hold values from 0 to 127, each once within a row
- step_index: int32 [2], P('scen'), may hold values from 0 to 5
Outputs:
- adjoint_out: float32 [2, 512, 512, 128], P('scen', 'tx', 'ty')
- grad_conductivity: float32 [512, 512, 128], P('tx', 'ty')
Inputs may be any that keep to these rules, and one draw needn't show every extreme that they name: Each row of holder names each of the 128 devices of tx+ty exactly once.
All inputs are finite; a program needn't handle non-finite values.
Results may differ from a plain program's by a relative error of at most 0.00002.
Values sent between devices are 32-bit elements; how exact they have to be, the bound alone decides.
A program may use at most 64 MiB of HBM per device.

v0:
```python
import jax
import jax.numpy as jnp
from jax import lax
from jax.sharding import PartitionSpec as P

step_size = 0.12


def padded_2(block, sides, width):
    for axis, dim in sides:
        count = lax.axis_size(axis)
        forward = [(i, i + 1) for i in range(count - 1)]
        backward = [(target, source) for source, target in forward]
        low = lax.ppermute(
            lax.slice_in_dim(block, block.shape[dim] - width, None, axis=dim), axis, forward
        )
        high = lax.ppermute(lax.slice_in_dim(block, 0, width, axis=dim), axis, backward)
        block = jnp.concatenate([low, block, high], axis=dim)
    return block


def flux_total(padded, cond_pad):
    face_x = (
        (cond_pad[1:, 1:-1] + cond_pad[:-1, 1:-1]) * 0.5 * (padded[1:, 1:-1] - padded[:-1, 1:-1])
    )
    total = face_x[1:] - face_x[:-1]
    face_y = (
        (cond_pad[1:-1, 1:] + cond_pad[1:-1, :-1]) * 0.5 * (padded[1:-1, 1:] - padded[1:-1, :-1])
    )
    total = total + face_y[:, 1:] - face_y[:, :-1]
    inner_field = padded[1:-1, 1:-1]
    inner_cond = cond_pad[1:-1, 1:-1]
    face_z = (
        (inner_cond[:, :, 1:] + inner_cond[:, :, :-1])
        * 0.5
        * (inner_field[:, :, 1:] - inner_field[:, :, :-1])
    )
    zero_pad = ((0, 0), (0, 0), (0, 1))
    left_pad = ((0, 0), (0, 0), (1, 0))
    return total + jnp.pad(face_z, zero_pad) - jnp.pad(face_z, left_pad)


def face_products(state_pad, adjoint_pad):
    prod_x = (state_pad[1:, 1:-1] - state_pad[:-1, 1:-1]) * (
        adjoint_pad[1:, 1:-1] - adjoint_pad[:-1, 1:-1]
    )
    total = prod_x[1:] + prod_x[:-1]
    prod_y = (state_pad[1:-1, 1:] - state_pad[1:-1, :-1]) * (
        adjoint_pad[1:-1, 1:] - adjoint_pad[1:-1, :-1]
    )
    total = total + prod_y[:, 1:] + prod_y[:, :-1]
    inner_state = state_pad[1:-1, 1:-1]
    inner_adjoint = adjoint_pad[1:-1, 1:-1]
    prod_z = (inner_state[:, :, 1:] - inner_state[:, :, :-1]) * (
        inner_adjoint[:, :, 1:] - inner_adjoint[:, :, :-1]
    )
    zero_pad = ((0, 0), (0, 0), (0, 1))
    left_pad = ((0, 0), (0, 0), (1, 0))
    total = total + jnp.pad(prod_z, zero_pad) + jnp.pad(prod_z, left_pad)
    return -0.5 * step_size * total


def state_halo(field):
    return padded_2(field, (("tx", 0), ("ty", 1)), 1)


def local(conductivity, cooling, source, adjoint_in, store, holder, step_index):
    cells_x, cells_y, cells_z = conductivity.shape
    chosen = lax.dynamic_index_in_dim(store[0, :, 0], step_index[0], 0, keepdims=False)
    arrived = lax.all_to_all(chosen, ("tx", "ty"), split_axis=0, concat_axis=0, tiled=True)
    state_zero = jnp.take(arrived, holder[0], axis=0).reshape(cells_x, cells_y, cells_z)
    cool_here = cooling[0]
    heat_here = source[0]
    adjoint_late = adjoint_in[0]
    near_coeffs = padded_2(jnp.stack([conductivity, adjoint_late]), (("tx", 1), ("ty", 2)), 1)
    cond_near = near_coeffs[0]
    late_near = near_coeffs[1]
    state_near = state_halo(state_zero)
    second_state = state_zero + step_size * (
        flux_total(state_near, cond_near) - cool_here * state_zero + heat_here
    )
    second_near = state_halo(second_state)
    middle_adjoint = adjoint_late + step_size * (
        flux_total(late_near, cond_near) - cool_here * adjoint_late
    )
    middle_near = state_halo(middle_adjoint)
    middle_inner = middle_near[1:-1, 1:-1]
    gradient = face_products(second_near, late_near) + face_products(state_near, middle_near)
    earliest = middle_inner + step_size * (
        flux_total(middle_near, cond_near) - cool_here * middle_inner
    )
    summed = lax.psum(gradient, "scen")
    return (earliest[None], summed)


def solution(mesh):
    in_specs = (
        P("tx", "ty", None),
        P("scen", "tx", "ty", None),
        P("scen", "tx", "ty", None),
        P("scen", "tx", "ty", None),
        P("scen", None, ("tx", "ty"), None, None),
        P(("tx", "ty"), None),
        P("scen"),
    )
    out_specs = (P("scen", "tx", "ty", None), P("tx", "ty", None))
    return jax.shard_map(local, mesh=mesh, in_specs=in_specs, out_specs=out_specs, check_vma=False)
```

profile of v0, /device:TPU:1, one launch (start us, length us, event | category | flops | bytes accessed | tf_op | source)
XLA Modules:
  0.0 168.9 jit_solution(16600107498923234903)
XLA Ops:
  7.8 1.3 constant_dynamic-slice_fusion
  9.1 1.7 %all_to_all.8 = f32[128,1,2048]{2,1,0:T(1,128)} reshape(f32[1,1,1,128,2048]{4,3,2,1,0:T(8,128)S(1)} %constant_dynamic-slice_fusion) | data formatting | bytes 2097152 | tf_op jit(solution)/shard_map/all_to_all | solution.py:70
  10.8 17.0 %all-to-all-start = ((f32[128,1,2048]{2,1,0:T(1,128)}), f32[128,1,2048]{2,1,0:T(1,128)}, u32[]{:S(2)}, u32[]{:S(2)}) async-start(f32[128,1,2048]{2,1,0:T(1,128)} %all_to_all.8), calls=%async_computation | async-start | bytes 2097152 | tf_op jit(solution)/shard_map/all_to_all | solution.py:70
  27.9 2.4 %collective-permute-start = (f32[2,1,32,128]{3,2,1,0:T(8,128)S(1)}, f32[2,1,32,128]{3,2,1,0:T(8,128)S(1)}, u32[]{:S(2)}, u32[]{:S(2)}) collective-permute-start(f32[2,1,32,128]{3,2,1,0:T(8,128)S(1)} %get-tuple-element.6), channel_id=1, source_target_pairs={{0,16},{16,32},{32,48},{48,64},{64,80},{80,96},{96,112},{1,17},{17... | collective-permute-start | bytes 98312 | tf_op jit(solution)/shard_map/ppermute | solution.py:14
  30.3 1.3 collective-permute-start.1
  33.2 2.7 %collective-permute-done.1 = f32[2,1,32,128]{3,2,1,0:T(8,128)S(1)} collective-permute-done((f32[2,1,32,128]{3,2,1,0:T(8,128)S(1)}, f32[2,1,32,128]{3,2,1,0:T(8,128)S(1)}, u32[]{:S(2)}, u32[]{:S(2)}) %collective-permute-start.1) | collective-permute-done | bytes 32800 | tf_op jit(solution)/shard_map/ppermute | solution.py:17
  36.1 3.4 %collective-permute-start.2 = (f32[2,66,1,128]{3,2,1,0:T(1,128)S(1)}, f32[2,66,1,128]{3,2,1,0:T(1,128)S(1)}, u32[]{:S(2)}, u32[]{:S(2)}) collective-permute-start(f32[2,66,1,128]{3,2,1,0:T(1,128)S(1)} %get-tuple-element.4), channel_id=1, source_target_pairs={{0,1},{1,2},{2,3},{3,4},{4,5},{5,6},{6,7},{7,8},{8,9},{9,10},{10,1... | collective-permute-start | bytes 202760 | tf_op jit(solution)/shard_map/ppermute | solution.py:14
  39.4 1.3 collective-permute-start.3
  40.8 7.5 %collective-permute-done.2 = f32[2,66,1,128]{3,2,1,0:T(1,128)S(1)} collective-permute-done((f32[2,66,1,128]{3,2,1,0:T(1,128)S(1)}, f32[2,66,1,128]{3,2,1,0:T(1,128)S(1)}, u32[]{:S(2)}, u32[]{:S(2)}) %collective-permute-start.2) | collective-permute-done | bytes 67616 | tf_op jit(solution)/shard_map/ppermute | solution.py:14
  48.2 2.4 %collective-permute-done.3 = f32[2,66,1,128]{3,2,1,0:T(1,128)S(1)} collective-permute-done((f32[2,66,1,128]{3,2,1,0:T(1,128)S(1)}, f32[2,66,1,128]{3,2,1,0:T(1,128)S(1)}, u32[]{:S(2)}, u32[]{:S(2)}) %collective-permute-start.3) | collective-permute-done | bytes 67616 | tf_op jit(solution)/shard_map/ppermute | solution.py:17
  52.4 5.2 %all-to-all-done = f32[128,1,2048]{2,1,0:T(1,128)} async-done(((f32[128,1,2048]{2,1,0:T(1,128)}), f32[128,1,2048]{2,1,0:T(1,128)}, u32[]{:S(2)}, u32[]{:S(2)}) %all-to-all-start) | async-done | bytes 1048608 | tf_op jit(solution)/shard_map/all_to_all | solution.py:70
  57.6 1.6 copy.15
  59.2 1.9 %gather_fusion = f32[128,2048]{1,0:T(8,128)} fusion(f32[128,2048]{1,0:T(8,128)S(1)} %bitcast.37, s32[1024]{0:T(1024)S(1)} %pad_clamp_fusion), kind=kCustom, calls=%fused_computation | custom fusion | bytes 2097664 | tf_op jit(solution)/shard_map/jit(_take)/gather | solution.py:71
  61.1 2.4 %gather.7 = f32[64,32,128]{2,1,0:T(8,128)} reshape(f32[128,2048]{1,0:T(8,128)} %gather_fusion) | data formatting | bytes 2097152 | tf_op jit(solution)/shard_map/jit(_take)/gather | solution.py:71
  63.7 1.3 collective-permute-start.8
  65.0 4.0 %collective-permute-start.9 = (f32[1,32,128]{2,1,0:T(8,128)S(1)}, f32[1,32,128]{2,1,0:T(8,128)S(1)}, u32[]{:S(2)}, u32[]{:S(2)}) collective-permute-start(f32[1,32,128]{2,1,0:T(8,128)S(1)} %slice.286), channel_id=1, source_target_pairs={{0,16},{16,32},{32,48},{48,64},{64,80},{80,96},{96,112},{1,17},{17... | collective-permute-start | bytes 49160 | tf_op jit(solution)/shard_map/ppermute | solution.py:14
  69.0 1.6 broadcast_select_fusion.1
  71.3 1.3 collective-permute-start.10
  72.6 4.0 %collective-permute-start.11 = (f32[66,1,128]{2,1,0:T(1,128)S(1)}, f32[66,1,128]{2,1,0:T(1,128)S(1)}, u32[]{:S(2)}, u32[]{:S(2)}) collective-permute-start(f32[66,1,128]{2,1,0:T(1,128)S(1)} %get-tuple-element.19), channel_id=1, source_target_pairs={{0,1},{1,2},{2,3},{3,4},{4,5},{5,6},{6,7},{7,8},{8,9},{9,10},{10,1... | collective-permute-start | bytes 101384 | tf_op jit(solution)/shard_map/ppermute | solution.py:14
  79.7 1.3 collective-permute-start.12
  81.0 4.0 %collective-permute-start.13 = (f32[1,32,128]{2,1,0:T(8,128)S(1)}, f32[1,32,128]{2,1,0:T(8,128)S(1)}, u32[]{:S(2)}, u32[]{:S(2)}) collective-permute-start(f32[1,32,128]{2,1,0:T(8,128)S(1)} %get-tuple-element.24), channel_id=1, source_target_pairs={{0,16},{16,32},{32,48},{48,64},{64,80},{80,96},{96,112},{1,17},{17... | collective-permute-start | bytes 49160 | tf_op jit(solution)/shard_map/ppermute | solution.py:14
  86.1 1.3 collective-permute-start.14
  87.4 4.0 %collective-permute-start.15 = (f32[66,1,128]{2,1,0:T(1,128)S(1)}, f32[66,1,128]{2,1,0:T(1,128)S(1)}, u32[]{:S(2)}, u32[]{:S(2)}) collective-permute-start(f32[66,1,128]{2,1,0:T(1,128)S(1)} %get-tuple-element.15), channel_id=1, source_target_pairs={{0,1},{1,2},{2,3},{3,4},{4,5},{5,6},{6,7},{7,8},{8,9},{9,10},{10,1... | collective-permute-start | bytes 101384 | tf_op jit(solution)/shard_map/ppermute | solution.py:14
  94.0 1.3 collective-permute-start.4
  95.3 4.1 %collective-permute-start.5 = (f32[1,32,128]{2,1,0:T(8,128)S(1)}, f32[1,32,128]{2,1,0:T(8,128)S(1)}, u32[]{:S(2)}, u32[]{:S(2)}) collective-permute-start(f32[1,32,128]{2,1,0:T(8,128)S(1)} %get-tuple-element.28), channel_id=1, source_target_pairs={{0,16},{16,32},{32,48},{48,64},{64,80},{80,96},{96,112},{1,17},{17... | collective-permute-start | bytes 49160 | tf_op jit(solution)/shard_map/ppermute | solution.py:14
  99.4 1.9 %fusion.38 = (f32[64,32,127]{2,1,0:T(8,128)S(1)}, f32[64,32,127]{2,1,0:T(8,128)}) fusion(f32[64,32,128]{2,1,0:T(8,128)S(1)} %fusion.31, f32[64,32,128]{2,1,0:T(8,128)S(1)} %broadcast_select_fusion.1, f32[66,34,128]{2,1,0:T(8,128)S(1)} %get-tuple-element.2), kind=kLoop, calls=%fused_computation.93 | loop fusion | flops 1560576 | bytes 8323072 | tf_op jit(solution)/shard_map/mul | solution.py:54
  102.7 4.5 %collective-permute-start.7 = (f32[66,1,128]{2,1,0:T(1,128)S(1)}, f32[66,1,128]{2,1,0:T(1,128)S(1)}, u32[]{:S(2)}, u32[]{:S(2)}) collective-permute-start(f32[66,1,128]{2,1,0:T(1,128)S(1)} %get-tuple-element.21), channel_id=1, source_target_pairs={{0,1},{1,2},{2,3},{3,4},{4,5},{5,6},{6,7},{7,8},{8,9},{9,10},{10,1... | collective-permute-start | bytes 101384 | tf_op jit(solution)/shard_map/ppermute | solution.py:14
  107.1 1.4 fusion.32
  109.0 1.9 %fusion.10 = f32[64,32,128]{2,1,0:T(8,128)} fusion(f32[64,33,128]{2,1,0:T(8,128)S(1)} %fusion.41, f32[65,32,128]{2,1,0:T(8,128)S(1)} %get-tuple-element.16, f32[64,33,128]{2,1,0:T(8,128)S(1)} %get-tuple-element.12, f32[65,32,128]{2,1,0:T(8,128)S(1)} %get-tuple-element.10, f32[64,32,127]{2,1,0:T(8,128)S(1)} %get-tuple-element.22, ...), kind=kLoop, calls=%fused_computation.40 | loop fusion | flops 3145728 | bytes 11517952 | tf_op jit(solution)/shard_map/add | solution.py:88
  112.8 1.7 %fusion.25 = f32[1,64,32,128]{3,2,1,0:T(8,128)} fusion(f32[64,32,128]{2,1,0:T(8,128)S(1)} %fusion.31, f32[64,33,128]{2,1,0:T(8,128)S(1)} %fusion.42, f32[65,32,128]{2,1,0:T(8,128)S(1)} %copy-done.7, f32[1,64,32,128]{3,2,1,0:T(8,128)S(1)} %copy-done.6, f32[64,32,127]{2,1,0:T(8,128)S(1)} %copy-done.8), kind=kLoop, calls=%fused_computation.67 | loop fusion | flops 2359296 | bytes 8380416 | tf_op jit(solution)/shard_map/broadcast_in_dim | solution.py:93
  114.5 45.3 %all-reduce.12.cloned.1.call-done = f32[64,32,128]{2,1,0:T(8,128)} async-done(((f32[64,32,128]{2,1,0:T(8,128)}), f32[64,32,128]{2,1,0:T(8,128)}) %all-reduce.12.cloned.1.call-update) | async-done | bytes 1048592 | tf_op jit(solution)/shard_map/psum | solution.py:92
  159.8 2.3 %copy.18 = f32[64,32,128]{2,1,0:T(8,128)} copy(f32[64,32,128]{2,1,0:T(8,128)} %all-reduce.12.cloned.1.call-done) | data formatting | bytes 2097152
  (71 shorter events, 14.6 us)
Async XLA Ops:
  10.8 17.1 %copy-start.1 = (f32[1,64,32,128]{3,2,1,0:T(8,128)S(1)}, f32[1,64,32,128]{3,2,1,0:T(8,128)}, u32[]{:S(2)}) copy-start(f32[1,64,32,128]{3,2,1,0:T(8,128)} %param.10) | copy-start | bytes 3145732
  10.8 17.1 %copy-start.3 = (f32[64,32,128]{2,1,0:T(8,128)S(1)}, f32[64,32,128]{2,1,0:T(8,128)}, u32[]{:S(2)}) copy-start(f32[64,32,128]{2,1,0:T(8,128)} %param.7) | copy-start | bytes 3145732
  10.8 46.8 %all-to-all-start = ((f32[128,1,2048]{2,1,0:T(1,128)}), f32[128,1,2048]{2,1,0:T(1,128)}, u32[]{:S(2)}, u32[]{:S(2)}) async-start(f32[128,1,2048]{2,1,0:T(1,128)} %all_to_all.8), calls=%async_computation | async-start | bytes 2097152 | tf_op jit(solution)/shard_map/all_to_all | solution.py:70
  27.8 4.3 %copy-start.10 = (s32[1,128]{1,0:T(1,128)S(1)}, s32[1,128]{1,0:T(1,128)}, u32[]{:S(2)}) copy-start(s32[1,128]{1,0:T(1,128)} %param.12) | copy-start | bytes 1540
  27.8 131.9 %all-reduce.12.cloned.1.call-start = ((), (), s32[]{:S(2)}) async-start(), calls=%async_computation.1 | async-start | bytes 2097152 | tf_op jit(solution)/shard_map/psum | solution.py:92
  27.9 5.3 %collective-permute-start = (f32[2,1,32,128]{3,2,1,0:T(8,128)S(1)}, f32[2,1,32,128]{3,2,1,0:T(8,128)S(1)}, u32[]{:S(2)}, u32[]{:S(2)}) collective-permute-start(f32[2,1,32,128]{3,2,1,0:T(8,128)S(1)} %get-tuple-element.6), channel_id=1, source_target_pairs={{0,16},{16,32},{32,48},{48,64},{64,80},{80,96},{96,112},{1,17},{17... | collective-permute-start | bytes 98312 | tf_op jit(solution)/shard_map/ppermute | solution.py:14
  30.3 5.6 %collective-permute-start.1 = (f32[2,1,32,128]{3,2,1,0:T(8,128)S(1)}, f32[2,1,32,128]{3,2,1,0:T(8,128)S(1)}, u32[]{:S(2)}, u32[]{:S(2)}) collective-permute-start(f32[2,1,32,128]{3,2,1,0:T(8,128)S(1)} %get-tuple-element.7), channel_id=1, source_target_pairs={{16,0},{32,16},{48,32},{64,48},{80,64},{96,80},{112,96},{17,1},{33... | collective-permute-start | bytes 98312 | tf_op jit(solution)/shard_map/ppermute | solution.py:17
  36.1 12.2 %collective-permute-start.2 = (f32[2,66,1,128]{3,2,1,0:T(1,128)S(1)}, f32[2,66,1,128]{3,2,1,0:T(1,128)S(1)}, u32[]{:S(2)}, u32[]{:S(2)}) collective-permute-start(f32[2,66,1,128]{3,2,1,0:T(1,128)S(1)} %get-tuple-element.4), channel_id=1, source_target_pairs={{0,1},{1,2},{2,3},{3,4},{4,5},{5,6},{6,7},{7,8},{8,9},{9,10},{10,1... | collective-permute-start | bytes 202760 | tf_op jit(solution)/shard_map/ppermute | solution.py:14
  39.4 11.2 %collective-permute-start.3 = (f32[2,66,1,128]{3,2,1,0:T(1,128)S(1)}, f32[2,66,1,128]{3,2,1,0:T(1,128)S(1)}, u32[]{:S(2)}, u32[]{:S(2)}) collective-permute-start(f32[2,66,1,128]{3,2,1,0:T(1,128)S(1)} %get-tuple-element.5), channel_id=1, source_target_pairs={{1,0},{2,1},{3,2},{4,3},{5,4},{6,5},{7,6},{8,7},{9,8},{10,9},{11,1... | collective-permute-start | bytes 202760 | tf_op jit(solution)/shard_map/ppermute | solution.py:17
  61.1 2.4 %copy-start.2 = (f32[128,2048]{1,0:T(8,128)S(1)}, f32[128,2048]{1,0:T(8,128)}, u32[]{:S(2)}) copy-start(f32[128,2048]{1,0:T(8,128)} %gather_fusion) | copy-start | bytes 3145732
  63.7 7.5 %collective-permute-start.8 = (f32[1,32,128]{2,1,0:T(8,128)S(1)}, f32[1,32,128]{2,1,0:T(8,128)S(1)}, u32[]{:S(2)}, u32[]{:S(2)}) collective-permute-start(f32[1,32,128]{2,1,0:T(8,128)S(1)} %slice.284), channel_id=1, source_target_pairs={{16,0},{32,16},{48,32},{64,48},{80,64},{96,80},{112,96},{17,1},{33... | collective-permute-start | bytes 49160 | tf_op jit(solution)/shard_map/ppermute | solution.py:17
  65.0 6.2 %collective-permute-start.9 = (f32[1,32,128]{2,1,0:T(8,128)S(1)}, f32[1,32,128]{2,1,0:T(8,128)S(1)}, u32[]{:S(2)}, u32[]{:S(2)}) collective-permute-start(f32[1,32,128]{2,1,0:T(8,128)S(1)} %slice.286), channel_id=1, source_target_pairs={{0,16},{16,32},{32,48},{48,64},{64,80},{80,96},{96,112},{1,17},{17... | collective-permute-start | bytes 49160 | tf_op jit(solution)/shard_map/ppermute | solution.py:14
  71.3 5.6 %collective-permute-start.10 = (f32[66,1,128]{2,1,0:T(1,128)S(1)}, f32[66,1,128]{2,1,0:T(1,128)S(1)}, u32[]{:S(2)}, u32[]{:S(2)}) collective-permute-start(f32[66,1,128]{2,1,0:T(1,128)S(1)} %get-tuple-element.18), channel_id=1, source_target_pairs={{1,0},{2,1},{3,2},{4,3},{5,4},{6,5},{7,6},{8,7},{9,8},{10,9},{11,1... | collective-permute-start | bytes 101384 | tf_op jit(solution)/shard_map/ppermute | solution.py:17
  72.6 5.0 %collective-permute-start.11 = (f32[66,1,128]{2,1,0:T(1,128)S(1)}, f32[66,1,128]{2,1,0:T(1,128)S(1)}, u32[]{:S(2)}, u32[]{:S(2)}) collective-permute-start(f32[66,1,128]{2,1,0:T(1,128)S(1)} %get-tuple-element.19), channel_id=1, source_target_pairs={{0,1},{1,2},{2,3},{3,4},{4,5},{5,6},{6,7},{7,8},{8,9},{9,10},{10,1... | collective-permute-start | bytes 101384 | tf_op jit(solution)/shard_map/ppermute | solution.py:14
  76.9 1.2 copy-start.4
  76.9 1.5 copy-start.5
  76.9 1.8 %copy-start.9 = (f32[1,64,32,128]{3,2,1,0:T(8,128)S(1)}, f32[1,64,32,128]{3,2,1,0:T(8,128)}, u32[]{:S(2)}) copy-start(f32[1,64,32,128]{3,2,1,0:T(8,128)} %param.9) | copy-start | bytes 3145732
  78.8 6.3 %copy-start = (f32[66,34,128]{2,1,0:T(8,128)S(1)}, f32[66,34,128]{2,1,0:T(8,128)}, u32[]{:S(2)}) copy-start(f32[66,34,128]{2,1,0:T(8,128)} %get-tuple-element.3) | copy-start | bytes 3446788
  79.7 6.3 %collective-permute-start.12 = (f32[1,32,128]{2,1,0:T(8,128)S(1)}, f32[1,32,128]{2,1,0:T(8,128)S(1)}, u32[]{:S(2)}, u32[]{:S(2)}) collective-permute-start(f32[1,32,128]{2,1,0:T(8,128)S(1)} %get-tuple-element.25), channel_id=1, source_target_pairs={{16,0},{32,16},{48,32},{64,48},{80,64},{96,80},{112,96},{17,1},{33... | collective-permute-start | bytes 49160 | tf_op jit(solution)/shard_map/ppermute | solution.py:17
  81.0 5.0 %collective-permute-start.13 = (f32[1,32,128]{2,1,0:T(8,128)S(1)}, f32[1,32,128]{2,1,0:T(8,128)S(1)}, u32[]{:S(2)}, u32[]{:S(2)}) collective-permute-start(f32[1,32,128]{2,1,0:T(8,128)S(1)} %get-tuple-element.24), channel_id=1, source_target_pairs={{0,16},{16,32},{32,48},{48,64},{64,80},{80,96},{96,112},{1,17},{17... | collective-permute-start | bytes 49160 | tf_op jit(solution)/shard_map/ppermute | solution.py:14
  86.1 5.8 %collective-permute-start.14 = (f32[66,1,128]{2,1,0:T(1,128)S(1)}, f32[66,1,128]{2,1,0:T(1,128)S(1)}, u32[]{:S(2)}, u32[]{:S(2)}) collective-permute-start(f32[66,1,128]{2,1,0:T(1,128)S(1)} %get-tuple-element.14), channel_id=1, source_target_pairs={{1,0},{2,1},{3,2},{4,3},{5,4},{6,5},{7,6},{8,7},{9,8},{10,9},{11,1... | collective-permute-start | bytes 101384 | tf_op jit(solution)/shard_map/ppermute | solution.py:17
  87.4 5.0 %collective-permute-start.15 = (f32[66,1,128]{2,1,0:T(1,128)S(1)}, f32[66,1,128]{2,1,0:T(1,128)S(1)}, u32[]{:S(2)}, u32[]{:S(2)}) collective-permute-start(f32[66,1,128]{2,1,0:T(1,128)S(1)} %get-tuple-element.15), channel_id=1, source_target_pairs={{0,1},{1,2},{2,3},{3,4},{4,5},{5,6},{6,7},{7,8},{8,9},{9,10},{10,1... | collective-permute-start | bytes 101384 | tf_op jit(solution)/shard_map/ppermute | solution.py:14
  94.0 7.3 %collective-permute-start.4 = (f32[1,32,128]{2,1,0:T(8,128)S(1)}, f32[1,32,128]{2,1,0:T(8,128)S(1)}, u32[]{:S(2)}, u32[]{:S(2)}) collective-permute-start(f32[1,32,128]{2,1,0:T(8,128)S(1)} %get-tuple-element.29), channel_id=1, source_target_pairs={{16,0},{32,16},{48,32},{64,48},{80,64},{96,80},{112,96},{17,1},{33... | collective-permute-start | bytes 49160 | tf_op jit(solution)/shard_map/ppermute | solution.py:17
  95.3 6.0 %collective-permute-start.5 = (f32[1,32,128]{2,1,0:T(8,128)S(1)}, f32[1,32,128]{2,1,0:T(8,128)S(1)}, u32[]{:S(2)}, u32[]{:S(2)}) collective-permute-start(f32[1,32,128]{2,1,0:T(8,128)S(1)} %get-tuple-element.28), channel_id=1, source_target_pairs={{0,16},{16,32},{32,48},{48,64},{64,80},{80,96},{96,112},{1,17},{17... | collective-permute-start | bytes 49160 | tf_op jit(solution)/shard_map/ppermute | solution.py:14
  101.4 7.2 %collective-permute-start.6 = (f32[66,1,128]{2,1,0:T(1,128)S(1)}, f32[66,1,128]{2,1,0:T(1,128)S(1)}, u32[]{:S(2)}, u32[]{:S(2)}) collective-permute-start(f32[66,1,128]{2,1,0:T(1,128)S(1)} %get-tuple-element.20), channel_id=1, source_target_pairs={{1,0},{2,1},{3,2},{4,3},{5,4},{6,5},{7,6},{8,7},{9,8},{10,9},{11,1... | collective-permute-start | bytes 101384 | tf_op jit(solution)/shard_map/ppermute | solution.py:17
  102.7 5.9 %collective-permute-start.7 = (f32[66,1,128]{2,1,0:T(1,128)S(1)}, f32[66,1,128]{2,1,0:T(1,128)S(1)}, u32[]{:S(2)}, u32[]{:S(2)}) collective-permute-start(f32[66,1,128]{2,1,0:T(1,128)S(1)} %get-tuple-element.21), channel_id=1, source_target_pairs={{0,1},{1,2},{2,3},{3,4},{4,5},{5,6},{6,7},{7,8},{8,9},{9,10},{10,1... | collective-permute-start | bytes 101384 | tf_op jit(solution)/shard_map/ppermute | solution.py:14
  110.9 1.2 copy-start.6
  110.9 1.5 copy-start.7
  110.9 1.8 %copy-start.8 = (f32[64,32,127]{2,1,0:T(8,128)S(1)}, f32[64,32,127]{2,1,0:T(8,128)}, u32[]{:S(2)}) copy-start(f32[64,32,127]{2,1,0:T(8,128)} %get-tuple-element.23) | copy-start | bytes 3121156
Sparse Core Ops, SparseCore 0:
  111.0 48.7 all-reduce.11
where the time goes:
time: 170 us; the launch traced here: 169 us
  waiting for transfers between devices  64.4 us (38%)
  starting transfers between devices  57.6 us (34%)
  other arithmetic  16.3 us (10%)
  local copies, waits for them, and re-layouts  15.4 us (9%)
  between operations  15.2 us (9%)
    psum x1, waiting for transfers between devices, local(): summed = lax.psum(gradient, 'scen')  45.3 us
    ppermute x8, starting transfers between devices, padded_2(): lax.ppermute(lax.slice_in_dim(block, block.shape[dim] - width, None, axis...  30.3 us
    all_to_all x1, starting transfers between devices, local(): lax.all_to_all(chosen, ('tx', 'ty'), split_axis=0, concat_axis=0, tiled=T...  17 us
    ppermute x8, starting transfers between devices, padded_2(): lax.ppermute(lax.slice_in_dim(block, 0, width, axis=dim), axis, backward)  10.3 us
    ppermute x8, waiting for transfers between devices, padded_2(): lax.ppermute(lax.slice_in_dim(block, block.shape[dim] - width, None, axis...  8.7 us
    unnamed x25, local copies, waits for them, and re-layouts  6.37 us
    all_to_all x1, waiting for transfers between devices, local(): lax.all_to_all(chosen, ('tx', 'ty'), split_axis=0, concat_axis=0, tiled=T...  5.23 us
    ppermute x8, waiting for transfers between devices, padded_2(): lax.ppermute(lax.slice_in_dim(block, 0, width, axis=dim), axis, backward)  5.18 us
  transfers between devices with their start and end apart: 18, of which 7 were waited for; matrix products, arithmetic and copies ran while one was open for 8% of the time, Pallas kernels for 0%

commit v1 on v0

--- a/solution.py
+++ b/solution.py
@@ -89,7 +89,7 @@
     earliest = middle_inner + step_size * (
         flux_total(middle_near, cond_near) - cool_here * middle_inner
     )
-    summed = lax.psum(gradient, "scen")
+    summed = jnp.sum(lax.all_gather(gradient, "scen"), axis=0)
     return (earliest[None], summed)
 
 

time: 170 us -> 156 us (0.918)
  waiting for transfers between devices: 64.4 us -> 49.9 us
  other arithmetic: 16.3 us -> 19.1 us
  local copies, waits for them, and re-layouts: 15.4 us -> 13.1 us
    psum x1 -> x0, waiting for transfers between devices: 45.3 us -> none  [local(): summed = lax.psum(gradient, 'scen')]
    all_gather x0 -> x1, waiting for transfers between devices: none -> 30.8 us  [local(): summed = jnp.sum(lax.all_gather(gradient, 'scen'), axis=0)]
    reduce_sum x0 -> x1, other arithmetic: none -> 2.86 us  [local(): summed = jnp.sum(lax.all_gather(gradient, 'scen'), axis=0)]
    unnamed x25 -> x24, local copies, waits for them, and re-layouts: 6.37 us -> 4.11 us
where the time goes in v1:
time: 156 us; the launch traced here: 155 us
  starting transfers between devices  57.6 us (37%)
  waiting for transfers between devices  49.9 us (32%)
  other arithmetic  19.1 us (12%)
  between operations  15.2 us (10%)
  local copies, waits for them, and re-layouts  13.1 us (8%)
    all_gather x1, waiting for transfers between devices, local(): summed = jnp.sum(lax.all_gather(gradient, 'scen'), axis=0)  30.8 us
    ppermute x8, starting transfers between devices, padded_2(): lax.ppermute(lax.slice_in_dim(block, block.shape[dim] - width, None, axis...  30.3 us
    all_to_all x1, starting transfers between devices, local(): lax.all_to_all(chosen, ('tx', 'ty'), split_axis=0, concat_axis=0, tiled=T...  17 us
    ppermute x8, starting transfers between devices, padded_2(): lax.ppermute(lax.slice_in_dim(block, 0, width, axis=dim), axis, backward)  10.3 us
    ppermute x8, waiting for transfers between devices, padded_2(): lax.ppermute(lax.slice_in_dim(block, block.shape[dim] - width, None, axis...  8.7 us
    all_to_all x1, waiting for transfers between devices, local(): lax.all_to_all(chosen, ('tx', 'ty'), split_axis=0, concat_axis=0, tiled=T...  5.23 us
    ppermute x8, waiting for transfers between devices, padded_2(): lax.ppermute(lax.slice_in_dim(block, 0, width, axis=dim), axis, backward)  5.18 us
    gather x2, local copies, waits for them, and re-layouts, local(): jnp.take(arrived, holder[0], axis=0).reshape(cells_x, cells_y, cells_z)  4.36 us
  transfers between devices with their start and end apart: 18, of which 7 were waited for; matrix products, arithmetic and copies ran while one was open for 8% of the time, Pallas kernels for 0%

profile of v1, /device:TPU:1, one launch (start us, length us, event | category | flops | bytes accessed | tf_op | source)
XLA Modules:
  0.0 155.0 jit_solution(3248901673391678837)
XLA Ops:
  7.8 1.3 constant_dynamic-slice_fusion
  9.1 1.7 %all_to_all.8 = f32[128,1,2048]{2,1,0:T(1,128)} reshape(f32[1,1,1,128,2048]{4,3,2,1,0:T(8,128)S(1)} %constant_dynamic-slice_fusion) | data formatting | bytes 2097152 | tf_op jit(solution)/shard_map/all_to_all | solution.py:70
  10.8 17.0 %all-to-all-start = ((f32[128,1,2048]{2,1,0:T(1,128)}), f32[128,1,2048]{2,1,0:T(1,128)}, u32[]{:S(2)}, u32[]{:S(2)}) async-start(f32[128,1,2048]{2,1,0:T(1,128)} %all_to_all.8), calls=%async_computation | async-start | bytes 2097152 | tf_op jit(solution)/shard_map/all_to_all | solution.py:70
  27.9 2.4 %collective-permute-start = (f32[2,1,32,128]{3,2,1,0:T(8,128)S(1)}, f32[2,1,32,128]{3,2,1,0:T(8,128)S(1)}, u32[]{:S(2)}, u32[]{:S(2)}) collective-permute-start(f32[2,1,32,128]{3,2,1,0:T(8,128)S(1)} %get-tuple-element.6), channel_id=1, source_target_pairs={{0,16},{16,32},{32,48},{48,64},{64,80},{80,96},{96,112},{1,17},{17... | collective-permute-start | bytes 98312 | tf_op jit(solution)/shard_map/ppermute | solution.py:14
  30.3 1.3 collective-permute-start.1
  33.2 2.7 %collective-permute-done.1 = f32[2,1,32,128]{3,2,1,0:T(8,128)S(1)} collective-permute-done((f32[2,1,32,128]{3,2,1,0:T(8,128)S(1)}, f32[2,1,32,128]{3,2,1,0:T(8,128)S(1)}, u32[]{:S(2)}, u32[]{:S(2)}) %collective-permute-start.1) | collective-permute-done | bytes 32800 | tf_op jit(solution)/shard_map/ppermute | solution.py:17
  36.1 3.4 %collective-permute-start.2 = (f32[2,66,1,128]{3,2,1,0:T(1,128)S(1)}, f32[2,66,1,128]{3,2,1,0:T(1,128)S(1)}, u32[]{:S(2)}, u32[]{:S(2)}) collective-permute-start(f32[2,66,1,128]{3,2,1,0:T(1,128)S(1)} %get-tuple-element.4), channel_id=1, source_target_pairs={{0,1},{1,2},{2,3},{3,4},{4,5},{5,6},{6,7},{7,8},{8,9},{9,10},{10,1... | collective-permute-start | bytes 202760 | tf_op jit(solution)/shard_map/ppermute | solution.py:14
  39.4 1.3 collective-permute-start.3
  40.8 7.5 %collective-permute-done.2 = f32[2,66,1,128]{3,2,1,0:T(1,128)S(1)} collective-permute-done((f32[2,66,1,128]{3,2,1,0:T(1,128)S(1)}, f32[2,66,1,128]{3,2,1,0:T(1,128)S(1)}, u32[]{:S(2)}, u32[]{:S(2)}) %collective-permute-start.2) | collective-permute-done | bytes 67616 | tf_op jit(solution)/shard_map/ppermute | solution.py:14
  48.2 2.4 %collective-permute-done.3 = f32[2,66,1,128]{3,2,1,0:T(1,128)S(1)} collective-permute-done((f32[2,66,1,128]{3,2,1,0:T(1,128)S(1)}, f32[2,66,1,128]{3,2,1,0:T(1,128)S(1)}, u32[]{:S(2)}, u32[]{:S(2)}) %collective-permute-start.3) | collective-permute-done | bytes 67616 | tf_op jit(solution)/shard_map/ppermute | solution.py:17
  52.4 5.2 %all-to-all-done = f32[128,1,2048]{2,1,0:T(1,128)} async-done(((f32[128,1,2048]{2,1,0:T(1,128)}), f32[128,1,2048]{2,1,0:T(1,128)}, u32[]{:S(2)}, u32[]{:S(2)}) %all-to-all-start) | async-done | bytes 1048608 | tf_op jit(solution)/shard_map/all_to_all | solution.py:70
  57.6 1.6 %copy.15 = f32[128,1,2048]{2,0,1:T(8,128)S(1)} copy(f32[128,1,2048]{2,1,0:T(1,128)} %all-to-all-done) | data formatting | bytes 2097152
  59.2 1.9 %gather_fusion = f32[128,2048]{1,0:T(8,128)} fusion(f32[128,2048]{1,0:T(8,128)S(1)} %bitcast.38, s32[1024]{0:T(1024)S(1)} %pad_clamp_fusion), kind=kCustom, calls=%fused_computation | custom fusion | bytes 2097664 | tf_op jit(solution)/shard_map/jit(_take)/gather | solution.py:71
  61.1 2.4 %gather.7 = f32[64,32,128]{2,1,0:T(8,128)} reshape(f32[128,2048]{1,0:T(8,128)} %gather_fusion) | data formatting | bytes 2097152 | tf_op jit(solution)/shard_map/jit(_take)/gather | solution.py:71
  63.7 1.3 collective-permute-start.8
  65.0 4.0 %collective-permute-start.9 = (f32[1,32,128]{2,1,0:T(8,128)S(1)}, f32[1,32,128]{2,1,0:T(8,128)S(1)}, u32[]{:S(2)}, u32[]{:S(2)}) collective-permute-start(f32[1,32,128]{2,1,0:T(8,128)S(1)} %slice.286), channel_id=1, source_target_pairs={{0,16},{16,32},{32,48},{48,64},{64,80},{80,96},{96,112},{1,17},{17... | collective-permute-start | bytes 49160 | tf_op jit(solution)/shard_map/ppermute | solution.py:14
  69.0 1.6 %broadcast_select_fusion.1 = f32[64,32,128]{2,1,0:T(8,128)S(1)} fusion(f32[64,32,128]{2,1,0:T(8,128)} %gather.7, pred[64,32]{1,0:T(8,128)(4,1)S(1)} %copy.12), kind=kLoop, calls=%fused_computation.89 | loop fusion | flops 262144 | bytes 2099200 | tf_op jit(solution)/shard_map/jit(_take)/select_n | solution.py:71
  71.3 1.3 collective-permute-start.10
  72.6 4.0 %collective-permute-start.11 = (f32[66,1,128]{2,1,0:T(1,128)S(1)}, f32[66,1,128]{2,1,0:T(1,128)S(1)}, u32[]{:S(2)}, u32[]{:S(2)}) collective-permute-start(f32[66,1,128]{2,1,0:T(1,128)S(1)} %get-tuple-element.19), channel_id=1, source_target_pairs={{0,1},{1,2},{2,3},{3,4},{4,5},{5,6},{6,7},{7,8},{8,9},{9,10},{10,1... | collective-permute-start | bytes 101384 | tf_op jit(solution)/shard_map/ppermute | solution.py:14
  79.7 1.3 collective-permute-start.12
  81.0 4.0 %collective-permute-start.13 = (f32[1,32,128]{2,1,0:T(8,128)S(1)}, f32[1,32,128]{2,1,0:T(8,128)S(1)}, u32[]{:S(2)}, u32[]{:S(2)}) collective-permute-start(f32[1,32,128]{2,1,0:T(8,128)S(1)} %get-tuple-element.24), channel_id=1, source_target_pairs={{0,16},{16,32},{32,48},{48,64},{64,80},{80,96},{96,112},{1,17},{17... | collective-permute-start | bytes 49160 | tf_op jit(solution)/shard_map/ppermute | solution.py:14
  86.1 1.3 collective-permute-start.14
  87.4 4.0 %collective-permute-start.15 = (f32[66,1,128]{2,1,0:T(1,128)S(1)}, f32[66,1,128]{2,1,0:T(1,128)S(1)}, u32[]{:S(2)}, u32[]{:S(2)}) collective-permute-start(f32[66,1,128]{2,1,0:T(1,128)S(1)} %get-tuple-element.15), channel_id=1, source_target_pairs={{0,1},{1,2},{2,3},{3,4},{4,5},{5,6},{6,7},{7,8},{8,9},{9,10},{10,1... | collective-permute-start | bytes 101384 | tf_op jit(solution)/shard_map/ppermute | solution.py:14
  94.0 1.3 collective-permute-start.4
  95.3 4.1 %collective-permute-start.5 = (f32[1,32,128]{2,1,0:T(8,128)S(1)}, f32[1,32,128]{2,1,0:T(8,128)S(1)}, u32[]{:S(2)}, u32[]{:S(2)}) collective-permute-start(f32[1,32,128]{2,1,0:T(8,128)S(1)} %get-tuple-element.28), channel_id=1, source_target_pairs={{0,16},{16,32},{32,48},{48,64},{64,80},{80,96},{96,112},{1,17},{17... | collective-permute-start | bytes 49160 | tf_op jit(solution)/shard_map/ppermute | solution.py:14
  99.4 1.9 %fusion.38 = (f32[64,32,127]{2,1,0:T(8,128)S(1)}, f32[64,32,127]{2,1,0:T(8,128)}) fusion(f32[64,32,128]{2,1,0:T(8,128)S(1)} %fusion.31, f32[64,32,128]{2,1,0:T(8,128)S(1)} %broadcast_select_fusion.1, f32[66,34,128]{2,1,0:T(8,128)S(1)} %get-tuple-element.2), kind=kLoop, calls=%fused_computation.93 | loop fusion | flops 1560576 | bytes 8323072 | tf_op jit(solution)/shard_map/mul | solution.py:54
  102.7 4.5 %collective-permute-start.7 = (f32[66,1,128]{2,1,0:T(1,128)S(1)}, f32[66,1,128]{2,1,0:T(1,128)S(1)}, u32[]{:S(2)}, u32[]{:S(2)}) collective-permute-start(f32[66,1,128]{2,1,0:T(1,128)S(1)} %get-tuple-element.21), channel_id=1, source_target_pairs={{0,1},{1,2},{2,3},{3,4},{4,5},{5,6},{6,7},{7,8},{8,9},{9,10},{10,1... | collective-permute-start | bytes 101384 | tf_op jit(solution)/shard_map/ppermute | solution.py:14
  107.1 1.4 fusion.32
  109.0 1.9 %fusion.10 = f32[64,32,128]{2,1,0:T(8,128)} fusion(f32[64,33,128]{2,1,0:T(8,128)S(1)} %fusion.41, f32[65,32,128]{2,1,0:T(8,128)S(1)} %get-tuple-element.16, f32[64,33,128]{2,1,0:T(8,128)S(1)} %get-tuple-element.12, f32[65,32,128]{2,1,0:T(8,128)S(1)} %get-tuple-element.10, f32[64,32,127]{2,1,0:T(8,128)S(1)} %get-tuple-element.22, ...), kind=kLoop, calls=%fused_computation.40 | loop fusion | flops 3145728 | bytes 11517952 | tf_op jit(solution)/shard_map/add | solution.py:88
  112.8 1.7 %fusion.25 = f32[1,64,32,128]{3,2,1,0:T(8,128)} fusion(f32[64,32,128]{2,1,0:T(8,128)S(1)} %fusion.31, f32[64,33,128]{2,1,0:T(8,128)S(1)} %fusion.42, f32[65,32,128]{2,1,0:T(8,128)S(1)} %copy-done.7, f32[1,64,32,128]{3,2,1,0:T(8,128)S(1)} %copy-done.6, f32[64,32,127]{2,1,0:T(8,128)S(1)} %copy-done.8), kind=kLoop, calls=%fused_computation.67 | loop fusion | flops 2359296 | bytes 8380416 | tf_op jit(solution)/shard_map/broadcast_in_dim | solution.py:93
  114.5 30.8 %all-gather.3.cloned.1.call-done = f32[128,32,128]{2,1,0:T(8,128)} async-done(((f32[64,32,128]{2,1,0:T(8,128)}), f32[128,32,128]{2,1,0:T(8,128)}) %all-gather.3.cloned.1.call-update) | async-done | bytes 2097168 | tf_op jit(solution)/shard_map/all_gather | solution.py:92
  145.3 2.9 %reduce_sum.9 = f32[64,32,128]{2,1,0:T(8,128)} reduce(f32[2,64,32,128]{3,2,1,0:T(8,128)} %bitcast.42, f32[]{:T(128)} %constant.13.clone.1), dimensions={0}, to_apply=%region_0.1 | reduce | flops 262144 | bytes 3145732 | tf_op jit(solution)/shard_map/reduce_sum | solution.py:92
  (71 shorter events, 14.6 us)
Async XLA Ops:
  10.8 17.1 %copy-start.1 = (f32[1,64,32,128]{3,2,1,0:T(8,128)S(1)}, f32[1,64,32,128]{3,2,1,0:T(8,128)}, u32[]{:S(2)}) copy-start(f32[1,64,32,128]{3,2,1,0:T(8,128)} %param.10) | copy-start | bytes 3145732
  10.8 17.1 %copy-start.3 = (f32[64,32,128]{2,1,0:T(8,128)S(1)}, f32[64,32,128]{2,1,0:T(8,128)}, u32[]{:S(2)}) copy-start(f32[64,32,128]{2,1,0:T(8,128)} %param.7) | copy-start | bytes 3145732
  10.8 46.8 %all-to-all-start = ((f32[128,1,2048]{2,1,0:T(1,128)}), f32[128,1,2048]{2,1,0:T(1,128)}, u32[]{:S(2)}, u32[]{:S(2)}) async-start(f32[128,1,2048]{2,1,0:T(1,128)} %all_to_all.8), calls=%async_computation | async-start | bytes 2097152 | tf_op jit(solution)/shard_map/all_to_all | solution.py:70
  27.8 4.3 %copy-start.10 = (s32[1,128]{1,0:T(1,128)S(1)}, s32[1,128]{1,0:T(1,128)}, u32[]{:S(2)}) copy-start(s32[1,128]{1,0:T(1,128)} %param.12) | copy-start | bytes 1540
  27.8 117.5 %all-gather.3.cloned.1.call-start = ((), (), s32[]{:S(2)}) async-start(), calls=%async_computation.1 | async-start | bytes 3145728 | tf_op jit(solution)/shard_map/all_gather | solution.py:92
  27.9 5.3 %collective-permute-start = (f32[2,1,32,128]{3,2,1,0:T(8,128)S(1)}, f32[2,1,32,128]{3,2,1,0:T(8,128)S(1)}, u32[]{:S(2)}, u32[]{:S(2)}) collective-permute-start(f32[2,1,32,128]{3,2,1,0:T(8,128)S(1)} %get-tuple-element.6), channel_id=1, source_target_pairs={{0,16},{16,32},{32,48},{48,64},{64,80},{80,96},{96,112},{1,17},{17... | collective-permute-start | bytes 98312 | tf_op jit(solution)/shard_map/ppermute | solution.py:14
  30.3 5.6 %collective-permute-start.1 = (f32[2,1,32,128]{3,2,1,0:T(8,128)S(1)}, f32[2,1,32,128]{3,2,1,0:T(8,128)S(1)}, u32[]{:S(2)}, u32[]{:S(2)}) collective-permute-start(f32[2,1,32,128]{3,2,1,0:T(8,128)S(1)} %get-tuple-element.7), channel_id=1, source_target_pairs={{16,0},{32,16},{48,32},{64,48},{80,64},{96,80},{112,96},{17,1},{33... | collective-permute-start | bytes 98312 | tf_op jit(solution)/shard_map/ppermute | solution.py:17
  36.1 12.2 %collective-permute-start.2 = (f32[2,66,1,128]{3,2,1,0:T(1,128)S(1)}, f32[2,66,1,128]{3,2,1,0:T(1,128)S(1)}, u32[]{:S(2)}, u32[]{:S(2)}) collective-permute-start(f32[2,66,1,128]{3,2,1,0:T(1,128)S(1)} %get-tuple-element.4), channel_id=1, source_target_pairs={{0,1},{1,2},{2,3},{3,4},{4,5},{5,6},{6,7},{7,8},{8,9},{9,10},{10,1... | collective-permute-start | bytes 202760 | tf_op jit(solution)/shard_map/ppermute | solution.py:14
  39.4 11.2 %collective-permute-start.3 = (f32[2,66,1,128]{3,2,1,0:T(1,128)S(1)}, f32[2,66,1,128]{3,2,1,0:T(1,128)S(1)}, u32[]{:S(2)}, u32[]{:S(2)}) collective-permute-start(f32[2,66,1,128]{3,2,1,0:T(1,128)S(1)} %get-tuple-element.5), channel_id=1, source_target_pairs={{1,0},{2,1},{3,2},{4,3},{5,4},{6,5},{7,6},{8,7},{9,8},{10,9},{11,1... | collective-permute-start | bytes 202760 | tf_op jit(solution)/shard_map/ppermute | solution.py:17
  61.1 2.4 %copy-start.2 = (f32[128,2048]{1,0:T(8,128)S(1)}, f32[128,2048]{1,0:T(8,128)}, u32[]{:S(2)}) copy-start(f32[128,2048]{1,0:T(8,128)} %gather_fusion) | copy-start | bytes 3145732
  63.7 7.5 %collective-permute-start.8 = (f32[1,32,128]{2,1,0:T(8,128)S(1)}, f32[1,32,128]{2,1,0:T(8,128)S(1)}, u32[]{:S(2)}, u32[]{:S(2)}) collective-permute-start(f32[1,32,128]{2,1,0:T(8,128)S(1)} %slice.284), channel_id=1, source_target_pairs={{16,0},{32,16},{48,32},{64,48},{80,64},{96,80},{112,96},{17,1},{33... | collective-permute-start | bytes 49160 | tf_op jit(solution)/shard_map/ppermute | solution.py:17
  65.0 6.2 %collective-permute-start.9 = (f32[1,32,128]{2,1,0:T(8,128)S(1)}, f32[1,32,128]{2,1,0:T(8,128)S(1)}, u32[]{:S(2)}, u32[]{:S(2)}) collective-permute-start(f32[1,32,128]{2,1,0:T(8,128)S(1)} %slice.286), channel_id=1, source_target_pairs={{0,16},{16,32},{32,48},{48,64},{64,80},{80,96},{96,112},{1,17},{17... | collective-permute-start | bytes 49160 | tf_op jit(solution)/shard_map/ppermute | solution.py:14
  71.3 5.6 %collective-permute-start.10 = (f32[66,1,128]{2,1,0:T(1,128)S(1)}, f32[66,1,128]{2,1,0:T(1,128)S(1)}, u32[]{:S(2)}, u32[]{:S(2)}) collective-permute-start(f32[66,1,128]{2,1,0:T(1,128)S(1)} %get-tuple-element.18), channel_id=1, source_target_pairs={{1,0},{2,1},{3,2},{4,3},{5,4},{6,5},{7,6},{8,7},{9,8},{10,9},{11,1... | collective-permute-start | bytes 101384 | tf_op jit(solution)/shard_map/ppermute | solution.py:17
  72.6 5.0 %collective-permute-start.11 = (f32[66,1,128]{2,1,0:T(1,128)S(1)}, f32[66,1,128]{2,1,0:T(1,128)S(1)}, u32[]{:S(2)}, u32[]{:S(2)}) collective-permute-start(f32[66,1,128]{2,1,0:T(1,128)S(1)} %get-tuple-element.19), channel_id=1, source_target_pairs={{0,1},{1,2},{2,3},{3,4},{4,5},{5,6},{6,7},{7,8},{8,9},{9,10},{10,1... | collective-permute-start | bytes 101384 | tf_op jit(solution)/shard_map/ppermute | solution.py:14
  76.9 1.2 copy-start.4
  76.9 1.5 copy-start.5
  76.9 1.8 %copy-start.9 = (f32[1,64,32,128]{3,2,1,0:T(8,128)S(1)}, f32[1,64,32,128]{3,2,1,0:T(8,128)}, u32[]{:S(2)}) copy-start(f32[1,64,32,128]{3,2,1,0:T(8,128)} %param.9) | copy-start | bytes 3145732
  78.8 6.3 %copy-start = (f32[66,34,128]{2,1,0:T(8,128)S(1)}, f32[66,34,128]{2,1,0:T(8,128)}, u32[]{:S(2)}) copy-start(f32[66,34,128]{2,1,0:T(8,128)} %get-tuple-element.3) | copy-start | bytes 3446788
  79.7 6.3 %collective-permute-start.12 = (f32[1,32,128]{2,1,0:T(8,128)S(1)}, f32[1,32,128]{2,1,0:T(8,128)S(1)}, u32[]{:S(2)}, u32[]{:S(2)}) collective-permute-start(f32[1,32,128]{2,1,0:T(8,128)S(1)} %get-tuple-element.25), channel_id=1, source_target_pairs={{16,0},{32,16},{48,32},{64,48},{80,64},{96,80},{112,96},{17,1},{33... | collective-permute-start | bytes 49160 | tf_op jit(solution)/shard_map/ppermute | solution.py:17
  81.0 5.0 %collective-permute-start.13 = (f32[1,32,128]{2,1,0:T(8,128)S(1)}, f32[1,32,128]{2,1,0:T(8,128)S(1)}, u32[]{:S(2)}, u32[]{:S(2)}) collective-permute-start(f32[1,32,128]{2,1,0:T(8,128)S(1)} %get-tuple-element.24), channel_id=1, source_target_pairs={{0,16},{16,32},{32,48},{48,64},{64,80},{80,96},{96,112},{1,17},{17... | collective-permute-start | bytes 49160 | tf_op jit(solution)/shard_map/ppermute | solution.py:14
  86.1 5.8 %collective-permute-start.14 = (f32[66,1,128]{2,1,0:T(1,128)S(1)}, f32[66,1,128]{2,1,0:T(1,128)S(1)}, u32[]{:S(2)}, u32[]{:S(2)}) collective-permute-start(f32[66,1,128]{2,1,0:T(1,128)S(1)} %get-tuple-element.14), channel_id=1, source_target_pairs={{1,0},{2,1},{3,2},{4,3},{5,4},{6,5},{7,6},{8,7},{9,8},{10,9},{11,1... | collective-permute-start | bytes 101384 | tf_op jit(solution)/shard_map/ppermute | solution.py:17
  87.4 5.0 %collective-permute-start.15 = (f32[66,1,128]{2,1,0:T(1,128)S(1)}, f32[66,1,128]{2,1,0:T(1,128)S(1)}, u32[]{:S(2)}, u32[]{:S(2)}) collective-permute-start(f32[66,1,128]{2,1,0:T(1,128)S(1)} %get-tuple-element.15), channel_id=1, source_target_pairs={{0,1},{1,2},{2,3},{3,4},{4,5},{5,6},{6,7},{7,8},{8,9},{9,10},{10,1... | collective-permute-start | bytes 101384 | tf_op jit(solution)/shard_map/ppermute | solution.py:14
  94.0 7.3 %collective-permute-start.4 = (f32[1,32,128]{2,1,0:T(8,128)S(1)}, f32[1,32,128]{2,1,0:T(8,128)S(1)}, u32[]{:S(2)}, u32[]{:S(2)}) collective-permute-start(f32[1,32,128]{2,1,0:T(8,128)S(1)} %get-tuple-element.29), channel_id=1, source_target_pairs={{16,0},{32,16},{48,32},{64,48},{80,64},{96,80},{112,96},{17,1},{33... | collective-permute-start | bytes 49160 | tf_op jit(solution)/shard_map/ppermute | solution.py:17
  95.3 6.0 %collective-permute-start.5 = (f32[1,32,128]{2,1,0:T(8,128)S(1)}, f32[1,32,128]{2,1,0:T(8,128)S(1)}, u32[]{:S(2)}, u32[]{:S(2)}) collective-permute-start(f32[1,32,128]{2,1,0:T(8,128)S(1)} %get-tuple-element.28), channel_id=1, source_target_pairs={{0,16},{16,32},{32,48},{48,64},{64,80},{80,96},{96,112},{1,17},{17... | collective-permute-start | bytes 49160 | tf_op jit(solution)/shard_map/ppermute | solution.py:14
  101.4 7.2 %collective-permute-start.6 = (f32[66,1,128]{2,1,0:T(1,128)S(1)}, f32[66,1,128]{2,1,0:T(1,128)S(1)}, u32[]{:S(2)}, u32[]{:S(2)}) collective-permute-start(f32[66,1,128]{2,1,0:T(1,128)S(1)} %get-tuple-element.20), channel_id=1, source_target_pairs={{1,0},{2,1},{3,2},{4,3},{5,4},{6,5},{7,6},{8,7},{9,8},{10,9},{11,1... | collective-permute-start | bytes 101384 | tf_op jit(solution)/shard_map/ppermute | solution.py:17
  102.7 5.9 %collective-permute-start.7 = (f32[66,1,128]{2,1,0:T(1,128)S(1)}, f32[66,1,128]{2,1,0:T(1,128)S(1)}, u32[]{:S(2)}, u32[]{:S(2)}) collective-permute-start(f32[66,1,128]{2,1,0:T(1,128)S(1)} %get-tuple-element.21), channel_id=1, source_target_pairs={{0,1},{1,2},{2,3},{3,4},{4,5},{5,6},{6,7},{7,8},{8,9},{9,10},{10,1... | collective-permute-start | bytes 101384 | tf_op jit(solution)/shard_map/ppermute | solution.py:14
  110.9 1.2 copy-start.6
  110.9 1.5 copy-start.7
  110.9 1.8 %copy-start.8 = (f32[64,32,127]{2,1,0:T(8,128)S(1)}, f32[64,32,127]{2,1,0:T(8,128)}, u32[]{:S(2)}) copy-start(f32[64,32,127]{2,1,0:T(8,128)} %get-tuple-element.23) | copy-start | bytes 3121156
Sparse Core Ops, SparseCore 0:
  111.0 34.2 all-gather.2
